TPU v7x, 32 devices: a whole 2x2x4 slice. The times are simulated.
32 devices in a mesh: span: 8 (over y, x, core), chord: 4 (over z).
Axes of the slice: x: 2, y: 2, z: 4, core: 2. Of those that a mesh axis runs over, the one named last changes fastest.
Arguments:
- adj_rhs: bfloat16 [16, 16, 320, 128], P('span', 'chord'), may hold values from -6 to 6
- diag_inv: bfloat16 [16, 16, 320, 320], P('span', 'chord'), may hold values from -0.3125 to 0.3125
- face_jac: bfloat16 [16, 16, 4, 80, 320], P('span', 'chord'), may hold values from -0.15625 to 0.15625
- face_mask: int32 [16, 16, 4], P('span', 'chord'), may hold values 0 or 1
- wall_map: int32 [16, 16, 16], P('span', 'chord'), may hold values from 0 to 255
- couple: float32 [6, 5], replicated, may hold values from -3 to 3
- shell_rhs: bfloat16 [2048, 6, 128], P(('span', 'chord')), may hold values from -6 to 6
- shell_inv: float32 [2048, 6, 6], P(('span', 'chord')), may hold values from -2.5 to 2.5
Outputs:
- fluid_adjoint: bfloat16 [16, 16, 320, 128], P('span', 'chord')
- shell_adjoint: bfloat16 [2048, 6, 128], P(('span', 'chord'))
All inputs are finite; a program needn't handle non-finite values. No bound on the sum of `face_mask` on one device may be relied on, other than what follows from the above.
Results may differ from a plain program's by a relative error of at most 0.0063.
Values may be sent and summed in bfloat16 or wider, within the bound.
A program may use at most 64 MiB of HBM per device.

v0:
```python
import jax
import jax.numpy as jnp
from jax import lax
from jax.sharding import PartitionSpec as P

NV = 5
ITERS = 3


def passed_along(block, axis, distance):
    devices = range(lax.axis_size(axis))
    route = [(i - distance, i) for i in devices if i - distance in devices]
    return lax.ppermute(block, axis, route)


def assemble(adj_rhs, low_span, high_span, low_chord, high_chord, wall_in):
    rows, cols, blk, width = adj_rhs.shape
    resid = adj_rhs.astype(jnp.float32).reshape(rows, cols, 4, 4, 4, NV, width)
    resid = resid.at[:, :, 0].add(
        -low_span.astype(jnp.float32).reshape(rows, cols, 4, 4, NV, width)
    )
    resid = resid.at[:, :, 3].add(
        -high_span.astype(jnp.float32).reshape(rows, cols, 4, 4, NV, width)
    )
    resid = resid.at[:, :, :, 0].add(
        -low_chord.astype(jnp.float32).reshape(rows, cols, 4, 4, NV, width)
    )
    resid = resid.at[:, :, :, 3].add(
        -high_chord.astype(jnp.float32).reshape(rows, cols, 4, 4, NV, width)
    )
    resid = resid.at[:, :, :, :, 0].add(-wall_in.reshape(rows, cols, 4, 4, NV, width))
    return resid.reshape(rows, cols, blk, width).astype(jnp.bfloat16)


def pass_span(moving, offset):
    rim_row = moving[-1:] if offset == 1 else moving[:1]
    arrived = passed_along(rim_row, "span", offset)
    if offset == 1:
        return jnp.concatenate([arrived, moving[:-1]], 0)
    return jnp.concatenate([moving[1:], arrived], 0)


def pass_chord(moving, offset):
    rim_col = moving[:, -1:] if offset == 1 else moving[:, :1]
    arrived = passed_along(rim_col, "chord", offset)
    if offset == 1:
        return jnp.concatenate([arrived, moving[:, :-1]], 1)
    return jnp.concatenate([moving[:, 1:], arrived], 1)


def face_terms(sent):
    low_span = pass_span(sent[:, :, 0], 1)
    high_span = pass_span(sent[:, :, 1], -1)
    low_chord = pass_chord(sent[:, :, 2], 1)
    high_chord = pass_chord(sent[:, :, 3], -1)
    return (low_span, high_span, low_chord, high_chord)


def per_device(adj_rhs, diag_inv, face_jac, face_mask, wall_map, couple, shell_rhs, shell_inv):
    high = lax.Precision.HIGHEST
    rows, cols, blk, width = adj_rhs.shape
    shell_count = shell_rhs.shape[0]
    chord_pos = lax.axis_index("chord")
    my_nodes = chord_pos * shell_count + lax.iota(jnp.int32, shell_count)
    wall_local = wall_map.reshape(-1)
    wall_count = wall_local.shape[0]
    strip_ids = lax.all_gather(wall_local, "chord", axis=0, tiled=True)
    fluid = jnp.einsum(
        "abmn,abnr->abmr", diag_inv, adj_rhs, preferred_element_type=jnp.float32
    ).astype(jnp.bfloat16)
    shell = jnp.einsum(
        "nst,ntr->nsr", shell_inv, shell_rhs.astype(jnp.float32), precision=high
    ).astype(jnp.bfloat16)
    weights = face_mask.astype(jnp.float32)[:, :, :, None, None]
    for step in range(1, ITERS):
        sent = jnp.einsum("abdmn,abnr->abdmr", face_jac, fluid, preferred_element_type=jnp.float32)
        sent = (sent * weights).astype(jnp.bfloat16)
        low_span, high_span, low_chord, high_chord = face_terms(sent)
        pick_piece = lax.all_gather(shell, "chord", axis=0, tiled=True)
        pick_count = pick_piece.shape[0]
        pick_hit = (wall_local[:, None] == lax.iota(jnp.int32, pick_count)[None, :]).astype(
            jnp.float32
        )
        picked = jnp.einsum("wn,nsr->wsr", pick_hit, pick_piece.astype(jnp.float32), precision=high)
        wall_in = jnp.einsum("sv,wsr->wvr", couple, picked, precision=high)
        wall_rows = fluid.reshape(rows, cols, 4, 4, 4, NV, width)[:, :, :, :, 0].reshape(
            wall_count, NV, width
        )
        piece = lax.all_gather(wall_rows, "chord", axis=0, tiled=True)
        hit = (my_nodes[:, None] == strip_ids[None, :]).astype(jnp.float32)
        summed = jnp.einsum("nw,wvr->nvr", hit, piece.astype(jnp.float32), precision=high)
        shell_load = jnp.einsum("sv,nvr->nsr", couple, summed, precision=high)
        wall_in, shell_load = (wall_in, shell_load)
        resid = assemble(adj_rhs, low_span, high_span, low_chord, high_chord, wall_in)
        fluid = jnp.einsum(
            "abmn,abnr->abmr", diag_inv, resid, preferred_element_type=jnp.float32
        ).astype(jnp.bfloat16)
        shell = jnp.einsum(
            "nst,ntr->nsr", shell_inv, shell_rhs.astype(jnp.float32) - shell_load, precision=high
        ).astype(jnp.bfloat16)
    return (fluid, shell)


def solution(mesh):
    return jax.shard_map(
        per_device,
        mesh=mesh,
        in_specs=(
            P("span", "chord", None, None),
            P("span", "chord", None, None),
            P("span", "chord", None, None, None),
            P("span", "chord", None),
            P("span", "chord", None),
            P(),
            P(("span", "chord"), None, None),
            P(("span", "chord"), None, None),
        ),
        out_specs=(P("span", "chord", None, None), P(("span", "chord"), None, None)),
        check_vma=False,
    )
```

profile of v0, /device:TPU:1, one launch (start us, length us, event | category | flops | bytes accessed | tf_op | source)
XLA Modules:
  0.0 125.1 jit_solution(14296814029680586999)
XLA Ops:
  0.6 0.8 convert_element_type.145
  1.5 0.7 copy-done
  2.2 1.9 %convolution_convert_fusion.2 = bf16[2,4,320,128]{3,2,1,0:T(8,128)(2,1)S(1)} fusion(bf16[2,4,320,320]{3,2,1,0:T(8,128)(2,1)S(1)} %copy-done, bf16[2,4,320,128]{3,2,1,0:T(8,128)(2,1)} %param.28), kind=kOutput, calls=%fused_computation.6 | convolution fusion | flops 210042880 | bytes 2949120 | tf_op jit(solution)/shard_map/abmn,abnr->abmr/dot_general | solution.py:68
  4.1 0.6 fusion.4
  4.8 0.7 fusion.48
  5.5 4.6 %collective-permute-start = (bf16[1,4,80,128]{3,2,1,0:T(8,128)(2,1)}, bf16[1,4,80,128]{3,2,1,0:T(8,128)(2,1)}, u32[]{:S(2)}, u32[]{:S(2)}) collective-permute-start(bf16[1,4,80,128]{3,2,1,0:T(8,128)(2,1)} %get-tuple-element.141), channel_id=1, source_target_pairs={{0,4},{4,8},{8,12},{12,16},{16,20},{20,24},{24,28},{1,5},{5,9},{9,... | collective-permute-start | bytes 245768 | tf_op jit(solution)/shard_map/ppermute | solution.py:13
  10.1 1.9 %collective-permute-start.1 = (bf16[1,4,80,128]{3,2,1,0:T(8,128)(2,1)}, bf16[1,4,80,128]{3,2,1,0:T(8,128)(2,1)}, u32[]{:S(2)}, u32[]{:S(2)}) collective-permute-start(bf16[1,4,80,128]{3,2,1,0:T(8,128)(2,1)} %get-tuple-element.139), channel_id=1, source_target_pairs={{4,0},{8,4},{12,8},{16,12},{20,16},{24,20},{28,24},{5,1},{9,5},{13... | collective-permute-start | bytes 245768 | tf_op jit(solution)/shard_map/ppermute | solution.py:13
  12.1 0.7 slice.554
  12.8 3.8 %collective-permute-start.2 = (bf16[2,1,80,128]{3,2,1,0:T(8,128)(2,1)}, bf16[2,1,80,128]{3,2,1,0:T(8,128)(2,1)}, u32[]{:S(2)}, u32[]{:S(2)}) collective-permute-start(bf16[2,1,80,128]{3,2,1,0:T(8,128)(2,1)} %slice.554), channel_id=1, source_target_pairs={{0,1},{1,2},{2,3},{4,5},{5,6},{6,7},{8,9},{9,10},{10,11},{12,13},{... | collective-permute-start | bytes 122888 | tf_op jit(solution)/shard_map/ppermute | solution.py:13
  16.6 0.6 slice.559
  17.2 1.3 %collective-permute-start.3 = (bf16[2,1,80,128]{3,2,1,0:T(8,128)(2,1)}, bf16[2,1,80,128]{3,2,1,0:T(8,128)(2,1)}, u32[]{:S(2)}, u32[]{:S(2)}) collective-permute-start(bf16[2,1,80,128]{3,2,1,0:T(8,128)(2,1)} %slice.559), channel_id=1, source_target_pairs={{1,0},{2,1},{3,2},{5,4},{6,5},{7,6},{9,8},{10,9},{11,10},{13,12},{... | collective-permute-start | bytes 122888 | tf_op jit(solution)/shard_map/ppermute | solution.py:13
  18.5 0.5 copy.150
  19.1 0.6 reshape.757
  19.7 0.2 copy.130
  19.9 0.4 convolution_convert_fusion.5
  20.3 14.9 %all_gather.15 = bf16[256,6,128]{2,0,1:T(8,128)(2,1)S(1)} all-gather(bf16[64,6,128]{2,0,1:T(8,128)(2,1)S(1)} %copy.132), channel_id=1, replica_groups=mesh['span'=8,'chord'=4] {'chord'}, dimensions={0}, use_global_device_ids=true | all-gather | bytes 491520 | tf_op jit(solution)/shard_map/all_gather | solution.py:79
  35.3 14.9 %all_gather.17 = bf16[512,5,128]{2,0,1:T(8,128)(2,1)S(1)} all-gather(bf16[128,5,128]{2,0,1:T(8,128)(2,1)S(1)} %bitcast.117), channel_id=1, replica_groups=mesh['span'=8,'chord'=4] {'chord'}, dimensions={0}, use_global_device_ids=true | all-gather | bytes 819200 | tf_op jit(solution)/shard_map/all_gather | solution.py:89
  50.2 7.0 %all-gather = s32[4,1,128]{2,1,0:T(1,128)S(1)} all-gather(s32[1,1,128]{2,1,0:T(1,128)S(1)} %copy-done.12), channel_id=1, replica_groups=mesh['span'=8,'chord'=4] {'chord'}, dimensions={0}, use_global_device_ids=true | all-gather | bytes 2560 | tf_op jit(solution)/shard_map/all_gather | solution.py:67
  57.2 0.2 fusion.29
  57.5 0.8 convolution_negate_fusion.1
  58.3 0.3 fusion.33
  58.6 0.5 fusion.6
  59.0 0.6 fusion.7
  59.6 11.6 %all_gather.18 = bf16[256,6,128]{2,0,1:T(8,128)(2,1)S(1)} all-gather(bf16[64,6,128]{2,0,1:T(8,128)(2,1)S(1)} %copy.154), channel_id=1, replica_groups=mesh['span'=8,'chord'=4] {'chord'}, dimensions={0}, use_global_device_ids=true | all-gather | bytes 491520 | tf_op jit(solution)/shard_map/all_gather | solution.py:79
  71.2 0.2 fusion.27
  71.5 0.8 convolution_negate_fusion
  72.3 0.5 copy.117
  72.9 0.3 copy-done.8
  73.3 0.1 copy.193
  73.4 0.8 copy-done.7
  74.2 0.1 copy.123
  74.4 0.1 copy.126
  74.6 0.8 copy.122
  75.5 0.8 copy.127
  76.4 0.9 copy.118
  77.3 0.1 add_dynamic-update-slice_fusion.1
  77.5 0.9 copy.121
  78.4 0.1 fusion.22
  78.5 0.3 fusion.21
  78.9 0.3 fusion.20
  79.2 0.4 fusion.19
  79.6 0.2 convert_element_type.153
  79.8 0.7 convolution_convert_fusion.1
  80.5 0.9 copy-done.2
  81.3 0.6 fusion.3
  82.1 12.8 %collective-permute-start.4 = (bf16[1,4,80,128]{3,2,1,0:T(8,128)(2,1)S(1)}, bf16[1,4,80,128]{3,2,1,0:T(8,128)(2,1)S(1)}, u32[]{:S(2)}, u32[]{:S(2)}) collective-permute-start(bf16[1,4,80,128]{3,2,1,0:T(8,128)(2,1)S(1)} %get-tuple-element.135), channel_id=1, source_target_pairs={{0,4},{4,8},{8,12},{12,16},{16,20},{20,24},{24,28},{1,5},{5,9},{9,... | collective-permute-start | bytes 245768 | tf_op jit(solution)/shard_map/ppermute | solution.py:13
  94.9 1.3 %collective-permute-start.6 = (bf16[2,1,80,128]{3,2,1,0:T(8,128)(2,1)S(1)}, bf16[2,1,80,128]{3,2,1,0:T(8,128)(2,1)S(1)}, u32[]{:S(2)}, u32[]{:S(2)}) collective-permute-start(bf16[2,1,80,128]{3,2,1,0:T(8,128)(2,1)S(1)} %slice.568), channel_id=1, source_target_pairs={{0,1},{1,2},{2,3},{4,5},{5,6},{6,7},{8,9},{9,10},{10,11},{12,13},{... | collective-permute-start | bytes 122888 | tf_op jit(solution)/shard_map/ppermute | solution.py:13
  96.2 1.3 %collective-permute-start.7 = (bf16[2,1,80,128]{3,2,1,0:T(8,128)(2,1)S(1)}, bf16[2,1,80,128]{3,2,1,0:T(8,128)(2,1)S(1)}, u32[]{:S(2)}, u32[]{:S(2)}) collective-permute-start(bf16[2,1,80,128]{3,2,1,0:T(8,128)(2,1)S(1)} %slice.573), channel_id=1, source_target_pairs={{1,0},{2,1},{3,2},{5,4},{6,5},{7,6},{9,8},{10,9},{11,10},{13,12},{... | collective-permute-start | bytes 122888 | tf_op jit(solution)/shard_map/ppermute | solution.py:13
  97.5 0.5 copy.159
  98.2 16.4 %all_gather.19 = bf16[512,5,128]{2,0,1:T(8,128)(2,1)S(1)} all-gather(bf16[128,5,128]{2,0,1:T(8,128)(2,1)S(1)} %bitcast.118), channel_id=1, replica_groups=mesh['span'=8,'chord'=4] {'chord'}, dimensions={0}, use_global_device_ids=true | all-gather | bytes 819200 | tf_op jit(solution)/shard_map/all_gather | solution.py:89
  114.5 0.3 fusion.31
  114.8 0.5 fusion.5
  115.2 0.6 fusion.8
  115.9 2.3 %collective-permute-start.5 = (bf16[1,4,80,128]{3,2,1,0:T(8,128)(2,1)S(1)}, bf16[1,4,80,128]{3,2,1,0:T(8,128)(2,1)S(1)}, u32[]{:S(2)}, u32[]{:S(2)}) collective-permute-start(bf16[1,4,80,128]{3,2,1,0:T(8,128)(2,1)S(1)} %get-tuple-element.133), channel_id=1, source_target_pairs={{4,0},{8,4},{12,8},{16,12},{20,16},{24,20},{28,24},{5,1},{9,5},{13... | collective-permute-start | bytes 245768 | tf_op jit(solution)/shard_map/ppermute | solution.py:13
  118.2 0.1 copy.142
  118.6 0.7 copy.163
  119.6 0.1 add_dynamic-update-slice_fusion
  119.7 2.5 %collective-permute-done.5 = bf16[1,4,80,128]{3,2,1,0:T(8,128)(2,1)S(1)} collective-permute-done((bf16[1,4,80,128]{3,2,1,0:T(8,128)(2,1)S(1)}, bf16[1,4,80,128]{3,2,1,0:T(8,128)(2,1)S(1)}, u32[]{:S(2)}, u32[]{:S(2)}) %collective-permute-start.5) | collective-permute-done | bytes 81952 | tf_op jit(solution)/shard_map/ppermute | solution.py:13
  122.2 0.1 fusion.18
  122.4 0.3 fusion.17
  122.7 0.3 fusion.16
  123.0 0.4 fusion.15
  123.4 0.2 convert_element_type.165
  123.6 1.5 %fusion.2 = bf16[2,4,320,128]{3,2,1,0:T(8,128)(2,1)} fusion(bf16[2,4,320,320]{3,2,1,0:T(8,128)(2,1)S(1)} %copy-done, bf16[2,4,320,128]{3,1,2,0:T(4,128)(2,1)S(1)} %bitcast.120), kind=kOutput, calls=%fused_computation.7 | convolution fusion | flops 210042880 | bytes 2949120 | tf_op jit(solution)/shard_map/abmn,abnr->abmr/dot_general | solution.py:95
  (63 shorter events, 1.5 us)
Async XLA Ops:
  0.6 1.6 %copy-start = (bf16[2,4,320,320]{3,2,1,0:T(8,128)(2,1)S(1)}, bf16[2,4,320,320]{3,2,1,0:T(8,128)(2,1)}, u32[]{:S(2)}) copy-start(bf16[2,4,320,320]{3,2,1,0:T(8,128)(2,1)} %param.29) | copy-start | bytes 4915204
  2.2 1.9 %copy-start.1 = (bf16[2,4,4,80,320]{4,3,2,1,0:T(8,128)(2,1)S(1)}, bf16[2,4,4,80,320]{4,3,2,1,0:T(8,128)(2,1)}, u32[]{:S(2)}) copy-start(bf16[2,4,4,80,320]{4,3,2,1,0:T(8,128)(2,1)} %param.30) | copy-start | bytes 4915204
  4.8 14.2 %copy-start.11 = (s32[2,4,16]{2,1,0:T(4,128)S(1)}, s32[2,4,16]{2,1,0:T(4,128)}, u32[]{:S(2)}) copy-start(s32[2,4,16]{2,1,0:T(4,128)} %param.32) | copy-start | bytes 1540
  4.8 14.9 %copy-start.10 = (f32[64,6,6]{0,2,1:T(8,128)S(1)}, f32[64,6,6]{0,2,1:T(8,128)}, u32[]{:S(2)}) copy-start(f32[64,6,6]{0,2,1:T(8,128)} %param.35) | copy-start | bytes 27652
  5.5 14.4 %copy-start.4 = (bf16[64,6,128]{2,0,1:T(8,128)(2,1)S(1)}, bf16[64,6,128]{2,0,1:T(8,128)(2,1)}, u32[]{:S(2)}) copy-start(bf16[64,6,128]{2,0,1:T(8,128)(2,1)} %param.34) | copy-start | bytes 294916
  5.5 70.9 %collective-permute-start = (bf16[1,4,80,128]{3,2,1,0:T(8,128)(2,1)}, bf16[1,4,80,128]{3,2,1,0:T(8,128)(2,1)}, u32[]{:S(2)}, u32[]{:S(2)}) collective-permute-start(bf16[1,4,80,128]{3,2,1,0:T(8,128)(2,1)} %get-tuple-element.141), channel_id=1, source_target_pairs={{0,4},{4,8},{8,12},{12,16},{16,20},{20,24},{24,28},{1,5},{5,9},{9,... | collective-permute-start | bytes 245768 | tf_op jit(solution)/shard_map/ppermute | solution.py:13
  10.1 67.3 %collective-permute-start.1 = (bf16[1,4,80,128]{3,2,1,0:T(8,128)(2,1)}, bf16[1,4,80,128]{3,2,1,0:T(8,128)(2,1)}, u32[]{:S(2)}, u32[]{:S(2)}) collective-permute-start(bf16[1,4,80,128]{3,2,1,0:T(8,128)(2,1)} %get-tuple-element.139), channel_id=1, source_target_pairs={{4,0},{8,4},{12,8},{16,12},{20,16},{24,20},{28,24},{5,1},{9,5},{13... | collective-permute-start | bytes 245768 | tf_op jit(solution)/shard_map/ppermute | solution.py:13
  12.1 8.2 %copy-start.5 = (bf16[2,4,80,128]{3,2,1,0:T(8,128)(2,1)}, bf16[2,4,80,128]{3,2,1,0:T(8,128)(2,1)S(1)}, u32[]{:S(2)}) copy-start(bf16[2,4,80,128]{3,2,1,0:T(8,128)(2,1)S(1)} %get-tuple-element.137) | copy-start | bytes 491524
  12.8 61.8 %collective-permute-start.2 = (bf16[2,1,80,128]{3,2,1,0:T(8,128)(2,1)}, bf16[2,1,80,128]{3,2,1,0:T(8,128)(2,1)}, u32[]{:S(2)}, u32[]{:S(2)}) collective-permute-start(bf16[2,1,80,128]{3,2,1,0:T(8,128)(2,1)} %slice.554), channel_id=1, source_target_pairs={{0,1},{1,2},{2,3},{4,5},{5,6},{6,7},{8,9},{9,10},{10,11},{12,13},{... | collective-permute-start | bytes 122888 | tf_op jit(solution)/shard_map/ppermute | solution.py:13
  17.2 58.3 %collective-permute-start.3 = (bf16[2,1,80,128]{3,2,1,0:T(8,128)(2,1)}, bf16[2,1,80,128]{3,2,1,0:T(8,128)(2,1)}, u32[]{:S(2)}, u32[]{:S(2)}) collective-permute-start(bf16[2,1,80,128]{3,2,1,0:T(8,128)(2,1)} %slice.559), channel_id=1, source_target_pairs={{1,0},{2,1},{3,2},{5,4},{6,5},{7,6},{9,8},{10,9},{11,10},{13,12},{... | collective-permute-start | bytes 122888 | tf_op jit(solution)/shard_map/ppermute | solution.py:13
  19.9 30.3 %copy-start.12 = (s32[1,1,128]{2,1,0:T(1,128)S(1)}, s32[1,1,128]{2,1,0:T(1,128)}, u32[]{:S(2)}) copy-start(s32[1,1,128]{2,1,0:T(1,128)} %reshape.757) | copy-start | bytes 1540
  20.3 37.2 %copy-start.9 = (f32[6,5]{1,0:T(8,128)S(1)}, f32[6,5]{1,0:T(8,128)}, u32[]{:S(2)}) copy-start(f32[6,5]{1,0:T(8,128)} %param.33) | copy-start | bytes 364
  59.6 12.7 %copy-start.3 = (bf16[2,4,320,128]{3,2,1,0:T(8,128)(2,1)S(1)}, bf16[2,4,320,128]{3,2,1,0:T(8,128)(2,1)}, u32[]{:S(2)}) copy-start(bf16[2,4,320,128]{3,2,1,0:T(8,128)(2,1)} %param.28) | copy-start | bytes 1966084
  71.5 1.4 %copy-start.6 = (bf16[2,4,80,128]{3,2,1,0:T(8,128)(2,1)S(1)}, bf16[2,4,80,128]{3,2,1,0:T(8,128)(2,1)}, u32[]{:S(2)}) copy-start(bf16[2,4,80,128]{3,2,1,0:T(8,128)(2,1)} %copy-done.5) | copy-start | bytes 491524
  72.3 0.9 copy-start.8
  73.2 0.9 copy-start.7
  79.8 1.5 %copy-start.2 = (bf16[2,4,4,80,320]{4,3,2,1,0:T(8,128)(2,1)S(1)}, bf16[2,4,4,80,320]{4,3,2,1,0:T(8,128)(2,1)}, u32[]{:S(2)}) copy-start(bf16[2,4,4,80,320]{4,3,2,1,0:T(8,128)(2,1)} %param.30) | copy-start | bytes 4915204
  82.1 37.5 %collective-permute-start.4 = (bf16[1,4,80,128]{3,2,1,0:T(8,128)(2,1)S(1)}, bf16[1,4,80,128]{3,2,1,0:T(8,128)(2,1)S(1)}, u32[]{:S(2)}, u32[]{:S(2)}) collective-permute-start(bf16[1,4,80,128]{3,2,1,0:T(8,128)(2,1)S(1)} %get-tuple-element.135), channel_id=1, source_target_pairs={{0,4},{4,8},{8,12},{12,16},{16,20},{20,24},{24,28},{1,5},{5,9},{9,... | collective-permute-start | bytes 245768 | tf_op jit(solution)/shard_map/ppermute | solution.py:13
  94.9 24.4 %collective-permute-start.6 = (bf16[2,1,80,128]{3,2,1,0:T(8,128)(2,1)S(1)}, bf16[2,1,80,128]{3,2,1,0:T(8,128)(2,1)S(1)}, u32[]{:S(2)}, u32[]{:S(2)}) collective-permute-start(bf16[2,1,80,128]{3,2,1,0:T(8,128)(2,1)S(1)} %slice.568), channel_id=1, source_target_pairs={{0,1},{1,2},{2,3},{4,5},{5,6},{6,7},{8,9},{9,10},{10,11},{12,13},{... | collective-permute-start | bytes 122888 | tf_op jit(solution)/shard_map/ppermute | solution.py:13
  96.2 23.2 %collective-permute-start.7 = (bf16[2,1,80,128]{3,2,1,0:T(8,128)(2,1)S(1)}, bf16[2,1,80,128]{3,2,1,0:T(8,128)(2,1)S(1)}, u32[]{:S(2)}, u32[]{:S(2)}) collective-permute-start(bf16[2,1,80,128]{3,2,1,0:T(8,128)(2,1)S(1)} %slice.573), channel_id=1, source_target_pairs={{1,0},{2,1},{3,2},{5,4},{6,5},{7,6},{9,8},{10,9},{11,10},{13,12},{... | collective-permute-start | bytes 122888 | tf_op jit(solution)/shard_map/ppermute | solution.py:13
  115.9 6.3 %collective-permute-start.5 = (bf16[1,4,80,128]{3,2,1,0:T(8,128)(2,1)S(1)}, bf16[1,4,80,128]{3,2,1,0:T(8,128)(2,1)S(1)}, u32[]{:S(2)}, u32[]{:S(2)}) collective-permute-start(bf16[1,4,80,128]{3,2,1,0:T(8,128)(2,1)S(1)} %get-tuple-element.133), channel_id=1, source_target_pairs={{4,0},{8,4},{12,8},{16,12},{20,16},{24,20},{28,24},{5,1},{9,5},{13... | collective-permute-start | bytes 245768 | tf_op jit(solution)/shard_map/ppermute | solution.py:13
where the time goes:
time: 126 us; the launch traced here: 125 us
  blocking collectives  64.7 us (51%)
  starting transfers between devices  29.3 us (23%)
  local copies, waits for them, and re-layouts  13 us (10%)
  matrix products  10.4 us (8%)
  other arithmetic  3.92 us (3%)
  waiting for transfers between devices  2.48 us (2%)
  between operations  1.35 us (1%)
    all_gather x2, blocking collectives, per_device(): piece = lax.all_gather(wall_rows, 'chord', axis=0, tiled=True)  31.2 us
    ppermute x8, starting transfers between devices, passed_along(): return lax.ppermute(block, axis, route)  29.3 us
    all_gather x2, blocking collectives, per_device(): pick_piece = lax.all_gather(shell, 'chord', axis=0, tiled=True)  26.5 us
    all_gather x1, blocking collectives, per_device(): strip_ids = lax.all_gather(wall_local, 'chord', axis=0, tiled=True)  7.02 us
    unnamed x30, local copies, waits for them, and re-layouts  4.28 us
    ppermute x8, local copies, waits for them, and re-layouts, passed_along(): return lax.ppermute(block, axis, route)  3.59 us
  transfers between devices with their start and end apart: 8, of which 1 were waited for; matrix products, arithmetic and copies ran while one was open for 11% of the time, Pallas kernels for 0%

commit v1 on v0

v1 whole, which is shorter than its diff:
```python
import functools

import jax
import jax.numpy as jnp
import numpy as np
from jax import lax
from jax.experimental import pallas as pl
from jax.experimental.pallas import tpu as pltpu
from jax.sharding import PartitionSpec as P

NV = 5
NF = 16
SDOF = 6
ITERS = 3
FACE = 80
BLK = 320
ROUNDS = ITERS - 1


def placement():
    m = np.arange(BLK)
    i, j, k, v = m // 80, (m // 20) % 4, (m // 5) % 4, m % 5
    out = np.zeros((BLK, 3 * FACE), np.float32)
    face = i * 20 + k * 5 + v
    low, high, wall = m[j == 0], m[j == 3], m[k == 0]
    out[low, face[low]] = 1
    out[high, FACE + face[high]] = 1
    out[wall, 2 * FACE + (v * NF + 4 * i + j)[wall]] = 1
    return out


def dot(a, b):
    return jnp.dot(a, b, preferred_element_type=jnp.float32)


def kernel(
    n_span, n_chord,
    couple, mask, wall_row, inv, rhs, place, pull, adj_h, diag_h, jac_h,
    fluid_out, shell_out,
    adj, diag, jac, fluid, low_span, high_span, low_chord, high_chord, span_out, chord_out,
    wall, part_out, part_in, csh, hot, hot_t,
    in_sem, ag_send, ag_recv, rs_send, rs_recv, face_send, face_recv,
):
    rows, cols = adj.shape[0], adj.shape[1]
    nodes = rhs.shape[1]
    width = rhs.shape[2]
    bf16, f32 = jnp.bfloat16, jnp.float32
    span, chord = lax.axis_index("span"), lax.axis_index("chord")
    elements = [(a, b) for a in range(rows) for b in range(cols)]
    mesh_id = pl.DeviceIdType.MESH

    loads = {}
    for a, b in elements:
        e = a * cols + b
        loads[a, b] = [
            pltpu.make_async_copy(adj_h.at[a, b], adj.at[a, b], in_sem.at[0, e]),
            pltpu.make_async_copy(diag_h.at[a, b], diag.at[a, b], in_sem.at[1, e]),
            pltpu.make_async_copy(jac_h.at[a, b], jac.at[a, b], in_sem.at[2, e]),
        ]
        for copy in loads[a, b]:
            copy.start()

    barrier = pltpu.get_barrier_semaphore()
    for k in range(1, n_chord):
        pl.semaphore_signal(
            barrier, inc=1, device_id=(span, lax.rem(chord + k, n_chord)), device_id_type=mesh_id
        )

    @pl.when(span > 0)
    def _():
        pl.semaphore_signal(barrier, inc=1, device_id=(span - 1, chord), device_id_type=mesh_id)

    @pl.when(span < n_span - 1)
    def _():
        pl.semaphore_signal(barrier, inc=1, device_id=(span + 1, chord), device_id_type=mesh_id)

    @pl.when(span == 0)
    def _():
        low_span[:, 0] = jnp.zeros_like(low_span[:, 0])

    @pl.when(span == n_span - 1)
    def _():
        high_span[:, rows - 1] = jnp.zeros_like(high_span[:, rows - 1])

    @pl.when(chord == 0)
    def _():
        low_chord[:, 0] = jnp.zeros_like(low_chord[:, 0])

    @pl.when(chord == n_chord - 1)
    def _():
        high_chord[:, cols - 1] = jnp.zeros_like(high_chord[:, cols - 1])

    walls = rows * cols * NF
    strip = n_chord * nodes
    node = lax.broadcasted_iota(jnp.int32, (strip, walls), 0)
    h = (node == wall_row[...]).astype(f32)
    hot[...] = h.astype(bf16)
    hot_t[...] = h.T.astype(bf16)

    def coup(s, v):
        return couple[s, v]

    def shell_of(load):
        x = [rhs[t].astype(f32) for t in range(SDOF)]
        if load is not None:
            x = [x[t] - load[t] for t in range(SDOF)]
        out = []
        for s in range(SDOF):
            acc = None
            for t in range(SDOF):
                term = inv[:, SDOF * s + t : SDOF * s + t + 1] * x[t]
                acc = term if acc is None else acc + term
            out.append(acc.astype(bf16))
        return out

    def ag_copy(r, k):
        return pltpu.make_async_remote_copy(
            src_ref=csh.at[r, chord],
            dst_ref=csh.at[r, chord],
            send_sem=ag_send.at[r, k],
            recv_sem=ag_recv.at[r, k],
            device_id=(span, lax.rem(chord + k, n_chord)),
            device_id_type=mesh_id,
        )

    def ag_wait(r):
        for k in range(1, n_chord):
            src = lax.rem(chord + n_chord - k, n_chord)
            pltpu.make_async_remote_copy(
                src_ref=csh.at[r, src],
                dst_ref=csh.at[r, src],
                send_sem=ag_send.at[r, k],
                recv_sem=ag_recv.at[r, k],
                device_id=(span, src),
                device_id_type=mesh_id,
            ).wait_recv()

    def gather_shell(r, shell):
        s32 = [s.astype(f32) for s in shell]
        for v in range(NV):
            acc = None
            for s in range(SDOF):
                term = coup(s, v) * s32[s]
                acc = term if acc is None else acc + term
            csh[r, chord, :, v * width : (v + 1) * width] = acc.astype(bf16)

    def rs_copy(r, k):
        to = lax.rem(chord + k, n_chord)
        return pltpu.make_async_remote_copy(
            src_ref=part_out.at[r, to],
            dst_ref=part_in.at[r, k],
            send_sem=rs_send.at[r, k],
            recv_sem=rs_recv.at[r, k],
            device_id=(span, to),
            device_id_type=mesh_id,
        )

    def send_parts(r):
        for c in range(n_chord):
            part_out[r, c] = dot(hot[c * nodes : (c + 1) * nodes], wall[...]).astype(bf16)
        for k in range(1, n_chord):
            rs_copy(r, k).start()

    def load_of(r):
        total = part_out[r, chord].astype(f32)
        for k in range(1, n_chord):
            rs_copy(r, k).wait_recv()
            total = total + part_in[r, k].astype(f32)
        load = []
        for s in range(SDOF):
            acc = None
            for v in range(NV):
                term = coup(s, v) * total[:, v * width : (v + 1) * width]
                acc = term if acc is None else acc + term
            load.append(acc)
        return load

    def face_copy(r, d):
        src = [span_out.at[r, 0], span_out.at[r, 1], chord_out.at[r, 0], chord_out.at[r, 1]][d]
        dst = [
            low_span.at[r, 0], high_span.at[r, rows - 1],
            low_chord.at[r, 0], high_chord.at[r, cols - 1],
        ][d]
        to = [(span + 1, chord), (span - 1, chord), (span, chord + 1), (span, chord - 1)][d]
        return pltpu.make_async_remote_copy(
            src_ref=src, dst_ref=dst,
            send_sem=face_send.at[r, d], recv_sem=face_recv.at[r, d],
            device_id=to, device_id_type=mesh_id,
        )

    sends = [span < n_span - 1, span > 0, chord < n_chord - 1, chord > 0]
    gets = [span > 0, span < n_span - 1, chord > 0, chord < n_chord - 1]

    def when_do(cond, do):
        @pl.when(cond)
        def _():
            do()

    def emit_faces(r, a, b, x):
        sent = dot(jac[a, b].reshape(BLK, BLK), x)
        face = [
            (sent[d * FACE : (d + 1) * FACE] * mask[a, b, d].astype(f32)).astype(bf16)
            for d in range(4)
        ]
        if a + 1 < rows:
            low_span[r, a + 1, b] = face[0]
        else:
            span_out[r, 0, b] = face[0]
        if a > 0:
            high_span[r, a - 1, b] = face[1]
        else:
            span_out[r, 1, b] = face[1]
        if b + 1 < cols:
            low_chord[r, b + 1, a] = face[2]
        else:
            chord_out[r, 0, a] = face[2]
        if b > 0:
            high_chord[r, b - 1, a] = face[3]
        else:
            chord_out[r, 1, a] = face[3]

    def emit_wall(a, b, x):
        rim = dot(pull[...], x).astype(bf16)
        e = a * cols + b
        for v in range(NV):
            wall[e * NF : (e + 1) * NF, v * width : (v + 1) * width] = rim[v * NF : (v + 1) * NF]

    def send_faces(r):
        for d in range(4):
            when_do(sends[d], lambda d=d: face_copy(r, d).start())

    def new_fluid(r, a, b, wall_in):
        e = a * cols + b
        rim = [
            wall_in[e * NF : (e + 1) * NF, v * width : (v + 1) * width] for v in range(NV)
        ]
        moved = dot(place[...], jnp.concatenate([low_chord[r, b, a], high_chord[r, b, a]] + rim, 0))
        x = adj[a, b].astype(f32) - moved
        x = jnp.concatenate(
            [
                x[:FACE] - low_span[r, a, b].astype(f32),
                x[FACE : BLK - FACE],
                x[BLK - FACE :] - high_span[r, a, b].astype(f32),
            ],
            0,
        )
        return dot(diag[a, b], x.astype(bf16)).astype(bf16)

    shell = shell_of(None)
    gather_shell(0, shell)
    pl.semaphore_wait(
        barrier,
        n_chord - 1 + (span > 0).astype(jnp.int32) + (span < n_span - 1).astype(jnp.int32),
    )
    for k in range(1, n_chord):
        ag_copy(0, k).start()

    for a, b in elements:
        loads[a, b][0].wait()
        loads[a, b][1].wait()
        x = dot(diag[a, b], adj[a, b]).astype(bf16)
        fluid[a, b] = x
        emit_wall(a, b, x)
    send_parts(0)
    for a, b in elements:
        loads[a, b][2].wait()
        emit_faces(0, a, b, fluid[a, b])
    send_faces(0)

    for r in range(ROUNDS):
        last = r == ROUNDS - 1
        if last:
            shell = shell_of(load_of(r))
            for s in range(SDOF):
                shell_out[s] = shell[s]
        ag_wait(r)
        wall_in = dot(hot_t[...], csh[r].reshape(strip, NV * width)).astype(bf16)
        for d in range(4):
            when_do(gets[d], lambda d=d: face_copy(r, d).wait_recv())
        for a, b in elements:
            x = new_fluid(r, a, b, wall_in)
            if last:
                fluid_out[a, b] = x
            else:
                fluid[a, b] = x
                emit_wall(a, b, x)
        if not last:
            send_parts(r + 1)
            for a, b in elements:
                emit_faces(r + 1, a, b, fluid[a, b])
            send_faces(r + 1)
            shell = shell_of(load_of(r))
            gather_shell(r + 1, shell)
            for k in range(1, n_chord):
                ag_copy(r + 1, k).start()

    for r in range(ROUNDS):
        for k in range(1, n_chord):
            ag_copy(r, k).wait_send()
            rs_copy(r, k).wait_send()
        for d in range(4):
            when_do(sends[d], lambda d=d: face_copy(r, d).wait_send())


def per_device(n_span, n_chord, adj_rhs, diag_inv, face_jac, face_mask, wall_map, couple, shell_rhs, shell_inv):
    rows, cols, blk, width = adj_rhs.shape
    nodes = shell_rhs.shape[0]
    walls = rows * cols * NF
    strip = n_chord * nodes
    bf16 = jnp.bfloat16
    place = placement()
    vmem = pl.BlockSpec(memory_space=pltpu.VMEM)
    smem = pl.BlockSpec(memory_space=pltpu.SMEM)
    hbm = pl.BlockSpec(memory_space=pl.ANY)
    sem = pltpu.SemaphoreType.DMA
    fluid, shell = pl.pallas_call(
        functools.partial(kernel, n_span, n_chord),
        out_shape=(
            jax.ShapeDtypeStruct((rows, cols, blk, width), bf16),
            jax.ShapeDtypeStruct((SDOF, nodes, width), bf16),
        ),
        in_specs=[smem, smem, vmem, vmem, vmem, vmem, vmem, hbm, hbm, hbm],
        out_specs=(vmem, vmem),
        scratch_shapes=[
            pltpu.VMEM((rows, cols, blk, width), bf16),
            pltpu.VMEM((rows, cols, blk, blk), bf16),
            pltpu.VMEM((rows, cols, 4, FACE, blk), bf16),
            pltpu.VMEM((rows, cols, blk, width), bf16),
            pltpu.VMEM((ROUNDS, rows, cols, FACE, width), bf16),
            pltpu.VMEM((ROUNDS, rows, cols, FACE, width), bf16),
            pltpu.VMEM((ROUNDS, cols, rows, FACE, width), bf16),
            pltpu.VMEM((ROUNDS, cols, rows, FACE, width), bf16),
            pltpu.VMEM((ROUNDS, 2, cols, FACE, width), bf16),
            pltpu.VMEM((ROUNDS, 2, rows, FACE, width), bf16),
            pltpu.VMEM((walls, NV * width), bf16),
            pltpu.VMEM((ROUNDS, n_chord, nodes, NV * width), bf16),
            pltpu.VMEM((ROUNDS, n_chord, nodes, NV * width), bf16),
            pltpu.VMEM((ROUNDS, n_chord, nodes, NV * width), bf16),
            pltpu.VMEM((strip, walls), bf16),
            pltpu.VMEM((walls, strip), bf16),
            sem((3, rows * cols)),
            sem((ROUNDS, n_chord)),
            sem((ROUNDS, n_chord)),
            sem((ROUNDS, n_chord)),
            sem((ROUNDS, n_chord)),
            sem((ROUNDS, 4)),
            sem((ROUNDS, 4)),
        ],
        compiler_params=pltpu.CompilerParams(
            collective_id=0, has_side_effects=True, vmem_limit_bytes=48 * 2**20
        ),
    )(
        couple,
        face_mask,
        wall_map.reshape(1, walls),
        shell_inv.reshape(nodes, SDOF * SDOF),
        shell_rhs.transpose(1, 0, 2),
        jnp.asarray(place, bf16),
        jnp.asarray(place[:, 2 * FACE :].T, bf16),
        adj_rhs,
        diag_inv,
        face_jac,
    )
    return fluid, shell.transpose(1, 0, 2)


def solution(mesh):
    return jax.shard_map(
        functools.partial(per_device, mesh.shape["span"], mesh.shape["chord"]),
        mesh=mesh,
        in_specs=(
            P("span", "chord", None, None),
            P("span", "chord", None, None),
            P("span", "chord", None, None, None),
            P("span", "chord", None),
            P("span", "chord", None),
            P(),
            P(("span", "chord"), None, None),
            P(("span", "chord"), None, None),
        ),
        out_specs=(P("span", "chord", None, None), P(("span", "chord"), None, None)),
        check_vma=False,
    )
```

time: 126 us -> 58.2 us (0.46)
  the two profiles are of different devices: /device:TPU:1 before, /device:TPU:0 now
where the time goes in v1:
time: 58.2 us; the launch traced here: 57.4 us
  Pallas kernels  45.5 us (78%)
  local copies, waits for them, and re-layouts  11.3 us (19%)
  between operations  0.65 us (1%)
    pallas_call x1, Pallas kernels, per_device(): pl.pallas_call(functools.partial(kernel, n_span, n_chord), out_shape=(jax...  45.5 us
    unnamed x18, local copies, waits for them, and re-layouts  9.66 us

profile of v1, /device:TPU:0, one launch (start us, length us, event | category | flops | bytes accessed | tf_op | source)
XLA Modules:
  0.0 57.4 jit_solution(11510171569017166763)
XLA Ops:
  0.6 0.8 %reshape.10.wall_row = s32[1,128]{1,0:T(1,128)S(1)} reshape(s32[2,4,16]{2,1,0:T(4,128)} %param.14) | data formatting | bytes 1024 | tf_op jit(solution)/shard_map/reshape | solution.py:355
  1.4 0.7 %reshape.11 = f32[64,36]{0,1:T(8,128)S(1)} reshape(f32[64,6,6]{0,2,1:T(8,128)} %param.17) | data formatting | bytes 18432 | tf_op jit(solution)/shard_map/reshape | solution.py:356
  2.1 0.1 copy.13.inv
  2.2 0.0 copy-start
  2.2 1.5 %copy-done = bf16[2,4,320,320]{3,2,1,0:T(8,128)(2,1)S(1)} copy-done((bf16[2,4,320,320]{3,2,1,0:T(8,128)(2,1)S(1)}, bf16[2,4,320,320]{3,2,1,0:T(8,128)(2,1)}, u32[]{:S(2)}) %copy-start) | copy-done | bytes 1638424
  3.8 0.0 copy-start.1
  3.8 1.5 %copy-done.1 = bf16[2,4,4,80,320]{4,3,2,1,0:T(8,128)(2,1)S(1)} copy-done((bf16[2,4,4,80,320]{4,3,2,1,0:T(8,128)(2,1)S(1)}, bf16[2,4,4,80,320]{4,3,2,1,0:T(8,128)(2,1)}, u32[]{:S(2)}) %copy-start.1) | copy-done | bytes 1638424
  5.3 0.0 copy-start.2
  5.3 1.1 %copy-done.2 = bf16[2,4,320,128]{3,2,1,0:T(8,128)(2,1)S(1)} copy-done((bf16[2,4,320,128]{3,2,1,0:T(8,128)(2,1)S(1)}, bf16[2,4,320,128]{3,2,1,0:T(8,128)(2,1)}, u32[]{:S(2)}) %copy-start.2) | copy-done | bytes 655384
  6.4 0.0 copy-start.3
  6.4 0.9 %copy-done.3 = bf16[320,240]{1,0:T(8,128)(2,1)S(1)} copy-done((bf16[320,240]{1,0:T(8,128)(2,1)S(1)}, bf16[320,240]{1,0:T(8,128)(2,1)}, u32[]{:S(2)}) %copy-start.3) | copy-done | bytes 153624
  7.3 0.0 copy-start.4
  7.3 0.9 %copy-done.4 = bf16[64,6,128]{2,0,1:T(8,128)(2,1)S(1)} copy-done((bf16[64,6,128]{2,0,1:T(8,128)(2,1)S(1)}, bf16[64,6,128]{2,0,1:T(8,128)(2,1)}, u32[]{:S(2)}) %copy-start.4) | copy-done | bytes 98328
  8.2 0.0 copy-start.5
  8.2 0.8 %copy-done.5 = bf16[80,320]{1,0:T(8,128)(2,1)S(1)} copy-done((bf16[80,320]{1,0:T(8,128)(2,1)S(1)}, bf16[80,320]{1,0:T(8,128)(2,1)}, u32[]{:S(2)}) %copy-start.5) | copy-done | bytes 51224
  9.1 0.0 copy-start.6
  9.1 0.7 %copy-done.6 = f32[6,5]{1,0:T(8,128)S(1)} copy-done((f32[6,5]{1,0:T(8,128)S(1)}, f32[6,5]{1,0:T(8,128)}, u32[]{:S(2)}) %copy-start.6) | copy-done | bytes 144
  9.7 0.0 copy-start.7
  9.7 0.7 %copy-done.7 = s32[2,4,4]{2,1,0:T(4,128)S(1)} copy-done((s32[2,4,4]{2,1,0:T(4,128)S(1)}, s32[2,4,4]{2,1,0:T(4,128)}, u32[]{:S(2)}) %copy-start.7) | copy-done | bytes 152
  10.4 45.5 %shard_map.113 = (bf16[2,4,320,128]{3,2,1,0:T(8,128)(2,1)S(1)}, bf16[6,64,128]{2,1,0:T(8,128)(2,1)S(1)}) custom-call(f32[6,5]{1,0:T(8,128)S(1)} %copy-done.6, s32[2,4,4]{2,1,0:T(4,128)S(1)} %copy-done.7, s32[1,128]{1,0:T(1,128)S(1)} %reshape.10.wall_row, f32[64,36]{1,0:T(8,128)S(1)} %copy.13.inv, bf16[6,64,128]{2,1,0:T(8,128)(2,1)S(1)} %bitcast.5, ...), custom_call_target="tpu_custom_call" | custom-call | tf_op jit(solution)/shard_map/pallas_call | solution.py:316
  55.9 0.8 %copy.16 = bf16[2,4,320,128]{3,2,1,0:T(8,128)(2,1)} copy(bf16[2,4,320,128]{3,2,1,0:T(8,128)(2,1)S(1)} %get-tuple-element.8) | data formatting | bytes 1310720
  56.8 0.6 %copy.17 = bf16[64,6,128]{2,0,1:T(8,128)(2,1)} copy(bf16[64,6,128]{2,0,1:T(8,128)(2,1)S(1)} %bitcast.4) | data formatting | bytes 196608
Async XLA Ops:
  2.2 1.5 %copy-start = (bf16[2,4,320,320]{3,2,1,0:T(8,128)(2,1)S(1)}, bf16[2,4,320,320]{3,2,1,0:T(8,128)(2,1)}, u32[]{:S(2)}) copy-start(bf16[2,4,320,320]{3,2,1,0:T(8,128)(2,1)} %diag_h.1) | copy-start | bytes 4915204
  3.8 1.5 %copy-start.1 = (bf16[2,4,4,80,320]{4,3,2,1,0:T(8,128)(2,1)S(1)}, bf16[2,4,4,80,320]{4,3,2,1,0:T(8,128)(2,1)}, u32[]{:S(2)}) copy-start(bf16[2,4,4,80,320]{4,3,2,1,0:T(8,128)(2,1)} %jac_h.1) | copy-start | bytes 4915204
  5.3 1.1 %copy-start.2 = (bf16[2,4,320,128]{3,2,1,0:T(8,128)(2,1)S(1)}, bf16[2,4,320,128]{3,2,1,0:T(8,128)(2,1)}, u32[]{:S(2)}) copy-start(bf16[2,4,320,128]{3,2,1,0:T(8,128)(2,1)} %adj_h.1) | copy-start | bytes 1966084
  6.4 0.9 %copy-start.3 = (bf16[320,240]{1,0:T(8,128)(2,1)S(1)}, bf16[320,240]{1,0:T(8,128)(2,1)}, u32[]{:S(2)}) copy-start(bf16[320,240]{1,0:T(8,128)(2,1)} %constant.4.clone.place) | copy-start | bytes 460804
  7.3 0.9 %copy-start.4 = (bf16[64,6,128]{2,0,1:T(8,128)(2,1)S(1)}, bf16[64,6,128]{2,0,1:T(8,128)(2,1)}, u32[]{:S(2)}) copy-start(bf16[64,6,128]{2,0,1:T(8,128)(2,1)} %param.16) | copy-start | bytes 294916
  8.2 0.8 %copy-start.5 = (bf16[80,320]{1,0:T(8,128)(2,1)S(1)}, bf16[80,320]{1,0:T(8,128)(2,1)}, u32[]{:S(2)}) copy-start(bf16[80,320]{1,0:T(8,128)(2,1)} %constant.5.clone.pull) | copy-start | bytes 153604
  9.1 0.7 %copy-start.6 = (f32[6,5]{1,0:T(8,128)S(1)}, f32[6,5]{1,0:T(8,128)}, u32[]{:S(2)}) copy-start(f32[6,5]{1,0:T(8,128)} %couple.1) | copy-start | bytes 364
  9.7 0.7 %copy-start.7 = (s32[2,4,4]{2,1,0:T(4,128)S(1)}, s32[2,4,4]{2,1,0:T(4,128)}, u32[]{:S(2)}) copy-start(s32[2,4,4]{2,1,0:T(4,128)} %mask.1) | copy-start | bytes 388

commit v2 on v1

--- a/solution.py
+++ b/solution.py
@@ -35,11 +35,11 @@
 
 def kernel(
     n_span, n_chord,
-    couple, mask, wall_row, inv, rhs, place, pull, adj_h, diag_h, jac_h,
+    couple, mask, wall_map, inv_t, rhs_h, place_h, pull_h, adj_h, diag_h, jac_h,
     fluid_out, shell_out,
-    adj, diag, jac, fluid, low_span, high_span, low_chord, high_chord, span_out, chord_out,
-    wall, part_out, part_in, csh, hot, hot_t,
-    in_sem, ag_send, ag_recv, rs_send, rs_recv, face_send, face_recv,
+    rhs, place, pull, adj, diag, jac, fluid, low_span, high_span, low_chord, high_chord, span_out, chord_out,
+    wall, own, part_out, part_in, csh, hot, hot_t,
+    small_sem, in_sem, ag_send, ag_recv, rs_send, rs_recv, face_send, face_recv,
 ):
     rows, cols = adj.shape[0], adj.shape[1]
     nodes = rhs.shape[1]
@@ -49,6 +49,10 @@
     elements = [(a, b) for a in range(rows) for b in range(cols)]
     mesh_id = pl.DeviceIdType.MESH
 
+    small = [
+        pltpu.make_async_copy(src, dst, small_sem.at[i])
+        for i, (src, dst) in enumerate([(rhs_h, rhs), (pull_h, pull), (place_h, place)])
+    ]
     loads = {}
     for a, b in elements:
         e = a * cols + b
@@ -57,14 +61,24 @@
             pltpu.make_async_copy(diag_h.at[a, b], diag.at[a, b], in_sem.at[1, e]),
             pltpu.make_async_copy(jac_h.at[a, b], jac.at[a, b], in_sem.at[2, e]),
         ]
-        for copy in loads[a, b]:
-            copy.start()
+    small[0].start()
+    small[1].start()
+    for a, b in elements:
+        loads[a, b][0].start()
+        loads[a, b][1].start()
+    for a, b in elements:
+        loads[a, b][2].start()
+    small[2].start()
 
     barrier = pltpu.get_barrier_semaphore()
-    for k in range(1, n_chord):
-        pl.semaphore_signal(
-            barrier, inc=1, device_id=(span, lax.rem(chord + k, n_chord)), device_id_type=mesh_id
-        )
+
+    @pl.when(chord > 0)
+    def _():
+        pl.semaphore_signal(barrier, inc=1, device_id=(span, chord - 1), device_id_type=mesh_id)
+
+    @pl.when(chord < n_chord - 1)
+    def _():
+        pl.semaphore_signal(barrier, inc=1, device_id=(span, chord + 1), device_id_type=mesh_id)
 
     @pl.when(span > 0)
     def _():
@@ -93,9 +107,28 @@
     walls = rows * cols * NF
     strip = n_chord * nodes
     node = lax.broadcasted_iota(jnp.int32, (strip, walls), 0)
-    h = (node == wall_row[...]).astype(f32)
+    ids = jnp.concatenate([wall_map[a] for a in range(rows)], 0)
+    lane = lax.broadcasted_iota(jnp.int32, (NF, walls), 1)
+    spread = (lax.broadcasted_iota(jnp.int32, (NF, walls), 0) == lane % NF).astype(bf16)
+    coarse = lax.shift_right_logical(ids, 3)
+    fine = ids - 8 * coarse
+    tiled = 8.0 * dot(coarse.astype(f32).astype(bf16), spread) + dot(fine.astype(f32).astype(bf16), spread)
+    element = lax.broadcasted_iota(jnp.int32, (rows * cols, walls), 0)
+    lane = lax.broadcasted_iota(jnp.int32, (rows * cols, walls), 1)
+    wall_row = jnp.sum(
+        jnp.where(lax.shift_right_logical(lane, 4) == element, tiled, 0.0), axis=0, keepdims=True
+    ).astype(jnp.int32)
+    h = (node == wall_row).astype(f32)
     hot[...] = h.astype(bf16)
     hot_t[...] = h.T.astype(bf16)
+
+    inv = jnp.concatenate(
+        [
+            jnp.concatenate([inv_t[s], jnp.zeros((8 - SDOF, nodes), f32)], 0)
+            for s in range(SDOF)
+        ],
+        0,
+    ).T
 
     def coup(s, v):
         return couple[s, v]
@@ -108,32 +141,56 @@
         for s in range(SDOF):
             acc = None
             for t in range(SDOF):
-                term = inv[:, SDOF * s + t : SDOF * s + t + 1] * x[t]
+                term = inv[:, 8 * s + t : 8 * s + t + 1] * x[t]
                 acc = term if acc is None else acc + term
             out.append(acc.astype(bf16))
         return out
 
-    def ag_copy(r, k):
+    def when_do(cond, do):
+        @pl.when(cond)
+        def _():
+            do()
+
+    has_low, has_high = chord > 0, chord < n_chord - 1
+
+    def ag_copy(r, way, s, block):
+        to = (span, chord + 1) if way == 0 else (span, chord - 1)
         return pltpu.make_async_remote_copy(
-            src_ref=csh.at[r, chord],
-            dst_ref=csh.at[r, chord],
-            send_sem=ag_send.at[r, k],
-            recv_sem=ag_recv.at[r, k],
-            device_id=(span, lax.rem(chord + k, n_chord)),
+            src_ref=csh.at[r, block],
+            dst_ref=csh.at[r, block],
+            send_sem=ag_send.at[r, way, s],
+            recv_sem=ag_recv.at[r, way, s],
+            device_id=to,
             device_id_type=mesh_id,
         )
 
-    def ag_wait(r):
-        for k in range(1, n_chord):
-            src = lax.rem(chord + n_chord - k, n_chord)
-            pltpu.make_async_remote_copy(
-                src_ref=csh.at[r, src],
-                dst_ref=csh.at[r, src],
-                send_sem=ag_send.at[r, k],
-                recv_sem=ag_recv.at[r, k],
-                device_id=(span, src),
-                device_id_type=mesh_id,
-            ).wait_recv()
+    def ag_held(s):
+        return chord - s, chord + s, chord >= s, chord + s < n_chord
+
+    def ag_start(r):
+        when_do(has_high, lambda: ag_copy(r, 0, 0, chord).start())
+        when_do(has_low, lambda: ag_copy(r, 1, 0, chord).start())
+
+    def ag_relay(r, s):
+        up, down, up_ok, down_ok = ag_held(s)
+
+        @pl.when(up_ok)
+        def _():
+            ag_copy(r, 0, s - 1, up).wait_recv()
+            if s < n_chord - 1:
+                when_do(has_high, lambda: ag_copy(r, 0, s, up).start())
+
+        @pl.when(down_ok)
+        def _():
+            ag_copy(r, 1, s - 1, down).wait_recv()
+            if s < n_chord - 1:
+                when_do(has_low, lambda: ag_copy(r, 1, s, down).start())
+
+    def ag_sent(r):
+        for s in range(n_chord - 1):
+            up, down, up_ok, down_ok = ag_held(s)
+            when_do(up_ok & has_high, lambda: ag_copy(r, 0, s, up).wait_send())
+            when_do(down_ok & has_low, lambda: ag_copy(r, 1, s, down).wait_send())
 
     def gather_shell(r, shell):
         s32 = [s.astype(f32) for s in shell]
@@ -144,28 +201,61 @@
                 acc = term if acc is None else acc + term
             csh[r, chord, :, v * width : (v + 1) * width] = acc.astype(bf16)
 
-    def rs_copy(r, k):
-        to = lax.rem(chord + k, n_chord)
+    def rs_copy(r, way, k):
         return pltpu.make_async_remote_copy(
-            src_ref=part_out.at[r, to],
-            dst_ref=part_in.at[r, k],
-            send_sem=rs_send.at[r, k],
-            recv_sem=rs_recv.at[r, k],
-            device_id=(span, to),
+            src_ref=part_out.at[r, way, k],
+            dst_ref=part_in.at[r, way, k],
+            send_sem=rs_send.at[r, way, k],
+            recv_sem=rs_recv.at[r, way, k],
+            device_id=(span, chord + 1) if way == 0 else (span, chord - 1),
             device_id_type=mesh_id,
         )
 
-    def send_parts(r):
+    def rs_start(r):
         for c in range(n_chord):
-            part_out[r, c] = dot(hot[c * nodes : (c + 1) * nodes], wall[...]).astype(bf16)
+            own[r, c] = dot(hot[c * nodes : (c + 1) * nodes], wall[...])
+        for k in range(n_chord - 1, 0, -1):
+
+            @pl.when(chord == 0)
+            def _():
+                part_out[r, 0, k] = own[r, k].astype(bf16)
+                rs_copy(r, 0, k).start()
+
+            @pl.when(chord == n_chord - 1)
+            def _():
+                part_out[r, 1, k] = own[r, n_chord - 1 - k].astype(bf16)
+                rs_copy(r, 1, k).start()
+
+    def rs_relay(r, k):
+        @pl.when((chord > 0) & (chord + k < n_chord))
+        def _():
+            rs_copy(r, 0, k + 1).wait_recv()
+            part_out[r, 0, k] = (own[r, chord + k] + part_in[r, 0, k + 1].astype(f32)).astype(bf16)
+            rs_copy(r, 0, k).start()
+
+        @pl.when((chord < n_chord - 1) & (chord >= k))
+        def _():
+            rs_copy(r, 1, k + 1).wait_recv()
+            part_out[r, 1, k] = (own[r, chord - k] + part_in[r, 1, k + 1].astype(f32)).astype(bf16)
+            rs_copy(r, 1, k).start()
+
+    def rs_sent(r):
         for k in range(1, n_chord):
-            rs_copy(r, k).start()
+            when_do(chord + k < n_chord, lambda: rs_copy(r, 0, k).wait_send())
+            when_do(chord >= k, lambda: rs_copy(r, 1, k).wait_send())
 
     def load_of(r):
-        total = part_out[r, chord].astype(f32)
-        for k in range(1, n_chord):
-            rs_copy(r, k).wait_recv()
-            total = total + part_in[r, k].astype(f32)
+        @pl.when(has_low)
+        def _():
+            rs_copy(r, 0, 1).wait_recv()
+            own[r, chord] = own[r, chord] + part_in[r, 0, 1].astype(f32)
+
+        @pl.when(has_high)
+        def _():
+            rs_copy(r, 1, 1).wait_recv()
+            own[r, chord] = own[r, chord] + part_in[r, 1, 1].astype(f32)
+
+        total = own[r, chord]
         load = []
         for s in range(SDOF):
             acc = None
@@ -190,11 +280,6 @@
 
     sends = [span < n_span - 1, span > 0, chord < n_chord - 1, chord > 0]
     gets = [span > 0, span < n_span - 1, chord > 0, chord < n_chord - 1]
-
-    def when_do(cond, do):
-        @pl.when(cond)
-        def _():
-            do()
 
     def emit_faces(r, a, b, x):
         sent = dot(jac[a, b].reshape(BLK, BLK), x)
@@ -246,60 +331,82 @@
         )
         return dot(diag[a, b], x.astype(bf16)).astype(bf16)
 
-    shell = shell_of(None)
-    gather_shell(0, shell)
-    pl.semaphore_wait(
-        barrier,
-        n_chord - 1 + (span > 0).astype(jnp.int32) + (span < n_span - 1).astype(jnp.int32),
-    )
-    for k in range(1, n_chord):
-        ag_copy(0, k).start()
-
-    for a, b in elements:
+    def faces_sent(r):
+        for d in range(4):
+            when_do(sends[d], lambda d=d: face_copy(r, d).wait_send())
+
+    small[0].wait()
+    gather_shell(0, shell_of(None))
+    greeted = [span > 0, span < n_span - 1, has_low, has_high]
+    pl.semaphore_wait(barrier, sum(c.astype(jnp.int32) for c in greeted))
+    ag_start(0)
+
+    relays = list(range(n_chord - 2, 0, -1))
+    half = (len(relays) + 1) // 2
+    hops = list(range(1, n_chord))
+
+    small[1].wait()
+    count = len(elements)
+    for e, (a, b) in enumerate(elements):
         loads[a, b][0].wait()
         loads[a, b][1].wait()
         x = dot(diag[a, b], adj[a, b]).astype(bf16)
         fluid[a, b] = x
         emit_wall(a, b, x)
-    send_parts(0)
-    for a, b in elements:
+    rs_start(0)
+    ag_relay(0, hops[0])
+    for e, (a, b) in enumerate(elements):
         loads[a, b][2].wait()
         emit_faces(0, a, b, fluid[a, b])
+        if e == count // 2 - 1 and len(hops) > 1:
+            ag_relay(0, hops[1])
     send_faces(0)
+    small[2].wait()
 
     for r in range(ROUNDS):
         last = r == ROUNDS - 1
-        if last:
-            shell = shell_of(load_of(r))
-            for s in range(SDOF):
-                shell_out[s] = shell[s]
-        ag_wait(r)
+        if r > 0:
+            for i in range(max(len(hops), len(relays))):
+                if i < len(relays):
+                    rs_relay(r, relays[i])
+                if i < len(hops):
+                    ag_relay(r, hops[i])
+        else:
+            for k in relays[:half]:
+                rs_relay(r, k)
+            for s in hops[2:]:
+                ag_relay(r, s)
         wall_in = dot(hot_t[...], csh[r].reshape(strip, NV * width)).astype(bf16)
         for d in range(4):
             when_do(gets[d], lambda d=d: face_copy(r, d).wait_recv())
-        for a, b in elements:
+        for e, (a, b) in enumerate(elements):
             x = new_fluid(r, a, b, wall_in)
             if last:
                 fluid_out[a, b] = x
             else:
                 fluid[a, b] = x
                 emit_wall(a, b, x)
+            if r == 0 and e == 1:
+                for k in relays[half:]:
+                    rs_relay(r, k)
+            if e == 5:
+                shell = shell_of(load_of(r))
+                if last:
+                    for s in range(SDOF):
+                        shell_out[s] = shell[s]
+                else:
+                    gather_shell(r + 1, shell)
+                    ag_start(r + 1)
         if not last:
-            send_parts(r + 1)
+            rs_start(r + 1)
             for a, b in elements:
                 emit_faces(r + 1, a, b, fluid[a, b])
             send_faces(r + 1)
-            shell = shell_of(load_of(r))
-            gather_shell(r + 1, shell)
-            for k in range(1, n_chord):
-                ag_copy(r + 1, k).start()
 
     for r in range(ROUNDS):
-        for k in range(1, n_chord):
-            ag_copy(r, k).wait_send()
-            rs_copy(r, k).wait_send()
-        for d in range(4):
-            when_do(sends[d], lambda d=d: face_copy(r, d).wait_send())
+        ag_sent(r)
+        rs_sent(r)
+        faces_sent(r)
 
 
 def per_device(n_span, n_chord, adj_rhs, diag_inv, face_jac, face_mask, wall_map, couple, shell_rhs, shell_inv):
@@ -319,9 +426,12 @@
             jax.ShapeDtypeStruct((rows, cols, blk, width), bf16),
             jax.ShapeDtypeStruct((SDOF, nodes, width), bf16),
         ),
-        in_specs=[smem, smem, vmem, vmem, vmem, vmem, vmem, hbm, hbm, hbm],
+        in_specs=[smem, smem, vmem, vmem, hbm, hbm, hbm, hbm, hbm, hbm],
         out_specs=(vmem, vmem),
         scratch_shapes=[
+            pltpu.VMEM((SDOF, nodes, width), bf16),
+            pltpu.VMEM((blk, 3 * FACE), bf16),
+            pltpu.VMEM((FACE, blk), bf16),
             pltpu.VMEM((rows, cols, blk, width), bf16),
             pltpu.VMEM((rows, cols, blk, blk), bf16),
             pltpu.VMEM((rows, cols, 4, FACE, blk), bf16),
@@ -333,27 +443,29 @@
             pltpu.VMEM((ROUNDS, 2, cols, FACE, width), bf16),
             pltpu.VMEM((ROUNDS, 2, rows, FACE, width), bf16),
             pltpu.VMEM((walls, NV * width), bf16),
-            pltpu.VMEM((ROUNDS, n_chord, nodes, NV * width), bf16),
-            pltpu.VMEM((ROUNDS, n_chord, nodes, NV * width), bf16),
+            pltpu.VMEM((ROUNDS, n_chord, nodes, NV * width), jnp.float32),
+            pltpu.VMEM((ROUNDS, 2, n_chord, nodes, NV * width), bf16),
+            pltpu.VMEM((ROUNDS, 2, n_chord, nodes, NV * width), bf16),
             pltpu.VMEM((ROUNDS, n_chord, nodes, NV * width), bf16),
             pltpu.VMEM((strip, walls), bf16),
             pltpu.VMEM((walls, strip), bf16),
+            sem((3,)),
             sem((3, rows * cols)),
-            sem((ROUNDS, n_chord)),
-            sem((ROUNDS, n_chord)),
-            sem((ROUNDS, n_chord)),
-            sem((ROUNDS, n_chord)),
+            sem((ROUNDS, 2, n_chord)),
+            sem((ROUNDS, 2, n_chord)),
+            sem((ROUNDS, 2, n_chord)),
+            sem((ROUNDS, 2, n_chord)),
             sem((ROUNDS, 4)),
             sem((ROUNDS, 4)),
         ],
         compiler_params=pltpu.CompilerParams(
-            collective_id=0, has_side_effects=True, vmem_limit_bytes=48 * 2**20
+            collective_id=0, has_side_effects=True, vmem_limit_bytes=60 * 2**20
         ),
     )(
         couple,
         face_mask,
-        wall_map.reshape(1, walls),
-        shell_inv.reshape(nodes, SDOF * SDOF),
+        wall_map,
+        shell_inv.transpose(1, 2, 0),
         shell_rhs.transpose(1, 0, 2),
         jnp.asarray(place, bf16),
         jnp.asarray(place[:, 2 * FACE :].T, bf16),

time: 58.2 us -> 45.6 us (0.78)
  local copies, waits for them, and re-layouts: 11.3 us -> 3.51 us
  Pallas kernels: 45.5 us -> 41.2 us
    unnamed x18 -> x2, local copies, waits for them, and re-layouts: 9.66 us -> 3.51 us
    pallas_call x1, Pallas kernels: 45.5 us -> 41.2 us  [per_device(): pl.pallas_call(functools.partial(kernel, n_span, n_chord), out_shape=(jax...]
    reshape x3 -> x0, local copies, waits for them, and re-layouts: 1.6 us -> none  [the longest x2 0.83 us: per_device(): shell_inv.reshape(nodes, SDOF * SDOF)]
where the time goes in v2:
time: 45.6 us; the launch traced here: 45.4 us
  Pallas kernels  41.2 us (90%)
  local copies, waits for them, and re-layouts  3.51 us (8%)
  between operations  0.64 us (1%)
    pallas_call x1, Pallas kernels, per_device(): pl.pallas_call(functools.partial(kernel, n_span, n_chord), out_shape=(jax...  41.2 us
    unnamed x2, local copies, waits for them, and re-layouts  3.51 us

profile of v2, /device:TPU:0, one launch (start us, length us, event | category | flops | bytes accessed | tf_op | source)
XLA Modules:
  0.0 45.4 jit_solution(12708907908187741327)
XLA Ops:
  0.6 41.2 %shard_map.113 = (bf16[2,4,320,128]{3,2,1,0:T(8,128)(2,1)}, bf16[6,64,128]{2,1,0:T(8,128)(2,1)}) custom-call(f32[6,5]{1,0:T(8,128)} %couple.1, s32[2,4,4]{2,1,0:T(4,128)} %mask.1, s32[2,4,16]{2,1,0:T(4,128)} %wall_map.1, f32[6,6,64]{2,1,0:T(8,128)} %bitcast.5, bf16[6,64,128]{2,1,0:T(8,128)(2,1)} %bitcast.4, bf16[320,240]{1,0:T(8,128)(2,1)} %constant.4.clone.place_h, ...), custom_call_target="tpu_custom_call" | custom-call | tf_op jit(solution)/shard_map/pallas_call | solution.py:423
  41.9 2.0 %copy.14 = bf16[2,4,320,128]{3,2,1,0:T(8,128)(2,1)} copy(bf16[2,4,320,128]{3,2,1,0:T(8,128)(2,1)} %get-tuple-element.8) | data formatting | bytes 1310720
  43.8 1.5 %copy.15 = bf16[64,6,128]{2,0,1:T(8,128)(2,1)} copy(bf16[64,6,128]{2,0,1:T(8,128)(2,1)} %bitcast.3) | data formatting | bytes 196608

commit v3 on v2

--- a/solution.py
+++ b/solution.py
@@ -214,19 +214,26 @@
     def rs_start(r):
         for c in range(n_chord):
             own[r, c] = dot(hot[c * nodes : (c + 1) * nodes], wall[...])
-        for k in range(n_chord - 1, 0, -1):
-
-            @pl.when(chord == 0)
-            def _():
-                part_out[r, 0, k] = own[r, k].astype(bf16)
-                rs_copy(r, 0, k).start()
-
-            @pl.when(chord == n_chord - 1)
-            def _():
-                part_out[r, 1, k] = own[r, n_chord - 1 - k].astype(bf16)
-                rs_copy(r, 1, k).start()
+        rs_end(r, n_chord - 1)
+
+    def rs_end(r, k):
+        @pl.when(chord == 0)
+        def _():
+            if k < n_chord - 1:
+                rs_copy(r, 0, k + 1).wait_send()
+            part_out[r, 0, k] = own[r, k].astype(bf16)
+            rs_copy(r, 0, k).start()
+
+        @pl.when(chord == n_chord - 1)
+        def _():
+            if k < n_chord - 1:
+                rs_copy(r, 1, k + 1).wait_send()
+            part_out[r, 1, k] = own[r, n_chord - 1 - k].astype(bf16)
+            rs_copy(r, 1, k).start()
 
     def rs_relay(r, k):
+        rs_end(r, k)
+
         @pl.when((chord > 0) & (chord + k < n_chord))
         def _():
             rs_copy(r, 0, k + 1).wait_recv()
@@ -241,8 +248,11 @@
 
     def rs_sent(r):
         for k in range(1, n_chord):
-            when_do(chord + k < n_chord, lambda: rs_copy(r, 0, k).wait_send())
-            when_do(chord >= k, lambda: rs_copy(r, 1, k).wait_send())
+            up, down = chord + k < n_chord, chord >= k
+            if k > 1:
+                up, down = up & has_low, down & has_high
+            when_do(up, lambda: rs_copy(r, 0, k).wait_send())
+            when_do(down, lambda: rs_copy(r, 1, k).wait_send())
 
     def load_of(r):
         @pl.when(has_low)

time: 45.6 us -> 44.5 us (0.976)
  Pallas kernels: 41.2 us -> 40.1 us
    pallas_call x1, Pallas kernels: 41.2 us -> 40.1 us  [per_device(): pl.pallas_call(functools.partial(kernel, n_span, n_chord), out_shape=(jax...]
where the time goes in v3:
time: 44.5 us; the launch traced here: 44.3 us
  Pallas kernels  40.1 us (90%)
  local copies, waits for them, and re-layouts  3.51 us (8%)
  between operations  0.64 us (1%)
    pallas_call x1, Pallas kernels, per_device(): pl.pallas_call(functools.partial(kernel, n_span, n_chord), out_shape=(jax...  40.1 us
    unnamed x2, local copies, waits for them, and re-layouts  3.51 us

profile of v3, /device:TPU:0, one launch (start us, length us, event | category | flops | bytes accessed | tf_op | source)
XLA Modules:
  0.0 44.3 jit_solution(12061212631175765833)
XLA Ops:
  0.6 40.1 %shard_map.113 = (bf16[2,4,320,128]{3,2,1,0:T(8,128)(2,1)}, bf16[6,64,128]{2,1,0:T(8,128)(2,1)}) custom-call(f32[6,5]{1,0:T(8,128)} %couple.1, s32[2,4,4]{2,1,0:T(4,128)} %mask.1, s32[2,4,16]{2,1,0:T(4,128)} %wall_map.1, f32[6,6,64]{2,1,0:T(8,128)} %bitcast.5, bf16[6,64,128]{2,1,0:T(8,128)(2,1)} %bitcast.4, bf16[320,240]{1,0:T(8,128)(2,1)} %constant.4.clone.place_h, ...), custom_call_target="tpu_custom_call" | custom-call | tf_op jit(solution)/shard_map/pallas_call | solution.py:433
  40.8 2.0 %copy.14 = bf16[2,4,320,128]{3,2,1,0:T(8,128)(2,1)} copy(bf16[2,4,320,128]{3,2,1,0:T(8,128)(2,1)} %get-tuple-element.8) | data formatting | bytes 1310720
  42.7 1.5 %copy.15 = bf16[64,6,128]{2,0,1:T(8,128)(2,1)} copy(bf16[64,6,128]{2,0,1:T(8,128)(2,1)} %bitcast.3) | data formatting | bytes 196608
